TPU v7x, 512 devices: a whole 4x8x8 slice. The times are simulated.
512 devices in a mesh: seq: 32 (over z_hi, x, core), head: 16 (over z_lo, y).
Axes of the slice: x: 4, y: 8, z: 8 (z_hi: 4, z_lo: 2; z = z_hi * 2 + z_lo), core: 2. Of those that a mesh axis runs over, the one named last changes fastest.
Arguments:
- queries: bfloat16 [1024, 128, 576], P('seq', 'head'), may hold values from -1024 to 1024
- latents: bfloat16 [4096, 576], P('seq'), may hold values from -6 to 6
- out_grad: bfloat16 [1024, 128, 512], P('seq', 'head'), may hold values from -6 to 6
- layer_out: bfloat16 [1024, 128, 512], P('seq', 'head'), may hold values from -4 to 4
- query_start: int32 [32], P('seq'), may hold values from 0 to 4095, as said below
Outputs:
- query_grad: bfloat16 [1024, 128, 576], P('seq', 'head')
- latent_grad: float32 [4096, 576], P(('seq', 'head'))
Inputs may be any that keep to these rules, and one draw needn't show every extreme that they name: Shard i holds the 32 queries at consecutive positions from query_start[i]; queries past the last latent position see every latent row.
All inputs are finite; a program needn't handle non-finite values.
Results may differ from a plain program's by a relative error of at most 0.0049.
Values may be sent and summed in bfloat16 or wider, within the bound.
No kernel may reach another device: no remote copies, remote signals or barrier semaphores. Data moves between devices by JAX's collectives and lax.ppermute only.
A program may use at most 64 MiB of HBM per device.

v0:
```python
import jax
import jax.numpy as jnp
from jax import lax
from jax.sharding import PartitionSpec as P

score_scale = 192 ** (-0.5)
masked_score = -1e30


def shifted(block, axis, distance):
    devices = range(lax.axis_size(axis))
    route = [((i - distance) % len(devices), i) for i in devices]
    return lax.ppermute(block, axis, route)


def visible_mask(first_key, key_rows, query_pos):
    key_pos = first_key + lax.iota(jnp.int32, key_rows)
    return key_pos[:, None] <= query_pos[None, :]


def score_block(block_rows, query_rows):
    return (
        lax.dot_general(
            block_rows, query_rows, (((1,), (1,)), ((), ())), preferred_element_type=jnp.float32
        )
        * score_scale
    )


def norm_step(running, block_rows, first_row, query_rows, query_pos):
    run_max, run_sum = running
    shown = visible_mask(first_row, block_rows.shape[0], query_pos)
    scores = jnp.where(shown, score_block(block_rows, query_rows), masked_score)
    new_max = jnp.maximum(run_max, jnp.max(scores, axis=0))
    weights = jnp.where(shown, jnp.exp(scores - new_max[None, :]), 0.0)
    run_sum = jnp.sum(weights, axis=0)
    return (new_max, run_sum)


def grad_block(block_rows, first_row, query_rows, grad_rows, row_delta, log_norm, query_pos):
    shown = visible_mask(first_row, block_rows.shape[0], query_pos)
    scores = score_block(block_rows, query_rows)
    weights = jnp.where(
        shown, jnp.exp(jnp.where(shown, scores - log_norm[None, :], masked_score)), 0.0
    )
    value_width = grad_rows.shape[1]
    prob_grad = lax.dot_general(
        block_rows[:, :value_width],
        grad_rows,
        (((1,), (1,)), ((), ())),
        preferred_element_type=jnp.float32,
    )
    dscore = (score_scale * weights * (prob_grad - row_delta[None, :])).astype(jnp.bfloat16)
    key_term = jnp.dot(dscore, query_rows, preferred_element_type=jnp.float32)
    value_term = jnp.dot(
        weights.astype(jnp.bfloat16), grad_rows, preferred_element_type=jnp.float32
    )
    key_term = key_term + jnp.pad(value_term, ((0, 0), (0, block_rows.shape[1] - value_width)))
    query_term = lax.dot_general(
        dscore, block_rows, (((0,), (0,)), ((), ())), preferred_element_type=jnp.float32
    )
    return (key_term, query_term)


def per_device(queries, latents, out_grad, layer_out, query_start):
    query_count, head_count, key_width = queries.shape
    row_count = query_count * head_count
    query_rows = queries.reshape(row_count, key_width)
    grad_rows = out_grad.reshape(row_count, out_grad.shape[2])
    row_delta = jnp.sum(
        out_grad.astype(jnp.float32) * layer_out.astype(jnp.float32), axis=2
    ).reshape(row_count)
    query_pos = query_start[0] + lax.iota(jnp.int32, row_count) // head_count
    key_count = latents.shape[0]
    cycle_size = lax.axis_size("seq")
    my_index = lax.axis_index("seq")
    start_state = (
        jnp.full((row_count,), masked_score, jnp.float32),
        jnp.zeros((row_count,), jnp.float32),
    )
    block_rows = lax.all_gather(latents, "seq", axis=0, tiled=True)
    running = start_state
    running = norm_step(running, block_rows, jnp.int32(0), query_rows, query_pos)
    add_stored = block_rows
    (run_max, run_sum), stored = (running, add_stored)
    log_norm = run_max + jnp.log(run_sum)

    def visit(first_row, rows, grad_sum, query_sum):
        block_rows = lax.dynamic_slice_in_dim(stored, first_row, rows, 0)
        key_term, query_term = grad_block(
            block_rows, first_row, query_rows, grad_rows, row_delta, log_norm, query_pos
        )
        return (grad_sum + key_term, query_sum + query_term)

    query_start_sum = jnp.zeros((row_count, key_width), jnp.float32)

    def cycle_turn(turn_index, state):
        grad_sum, query_sum = state
        owner_index = (my_index - turn_index - 1) % cycle_size
        grad_sum, query_sum = visit(owner_index * key_count, key_count, grad_sum, query_sum)
        return (shifted(grad_sum, "seq", 1), query_sum)

    start_sum = jnp.zeros((key_count, key_width), jnp.float32)
    grad_sum, query_sum = lax.fori_loop(0, cycle_size - 1, cycle_turn, (start_sum, query_start_sum))
    owned_sum, query_sum = visit(my_index * key_count, key_count, grad_sum, query_sum)
    latent_grad = lax.psum_scatter(owned_sum, "head", scatter_dimension=0, tiled=True)
    query_grad = query_sum.astype(jnp.bfloat16).reshape(query_count, head_count, key_width)
    return (query_grad, latent_grad)


def solution(mesh):
    placed = (
        P("seq", "head", None),
        P("seq", None),
        P("seq", "head", None),
        P("seq", "head", None),
        P("seq"),
    )
    return jax.shard_map(
        per_device,
        mesh=mesh,
        in_specs=placed,
        out_specs=(P("seq", "head", None), P(("seq", "head"), None)),
        check_vma=False,
    )
```

profile of v0, /device:TPU:2, one launch (start us, length us, event | category | flops | bytes accessed | tf_op | source)
XLA Modules:
  0.0 738.1 jit_solution(2161569260429799532)
XLA Ops:
  11.1 75.9 %all-gather.2.cloned.1.call-done = bf16[4096,576]{1,0:T(8,128)(2,1)} async-done(((bf16[128,576]{1,0:T(8,128)(2,1)}), bf16[4096,576]{1,0:T(8,128)(2,1)}) %all-gather.2.cloned.1.call-update) | async-done | bytes 4718608 | tf_op jit(solution)/shard_map/all_gather | solution.py:81
  94.0 479.8 %while.19 = (s32[]{:T(128)}, f32[128,576]{0,1:T(8,128)S(1)}, f32[256,576]{0,1:T(8,128)S(1)}, s32[]{:T(128)}, bf16[4096,576]{1,0:T(8,128)(2,1)}, /*index=5*/bf16[...) while((s32[]{:T(128)}, f32[128,576]{0,1:T(8,128)S(1)}, ...), condition=%wide.wide.region_4.5_spmd.clone, body=%wide.wide.region_3.4_spmd.clone.sunk | while | flops 181127568 | bytes 5641630 | solution.py:104
  124.1 4.8 collective-permute-done
  135.7 8.6 %collective-permute-done = f32[128,576]{0,1:T(8,128)S(1)} collective-permute-done((f32[128,576]{0,1:T(8,128)S(1)}, f32[128,576]{0,1:T(8,128)S(1)}, u32[]{:S(2)}, u32[]{:S(2)}) %collective-permute-start) | collective-permute-done | bytes 294944 | tf_op jit(solution)/shard_map/while/body/eval_jaxpr/ppermute | solution.py:13
  151.1 9.0 %collective-permute-done = f32[128,576]{0,1:T(8,128)S(1)} collective-permute-done((f32[128,576]{0,1:T(8,128)S(1)}, f32[128,576]{0,1:T(8,128)S(1)}, u32[]{:S(2)}, u32[]{:S(2)}) %collective-permute-start) | collective-permute-done | bytes 294944 | tf_op jit(solution)/shard_map/while/body/eval_jaxpr/ppermute | solution.py:13
  167.0 9.0 %collective-permute-done = f32[128,576]{0,1:T(8,128)S(1)} collective-permute-done((f32[128,576]{0,1:T(8,128)S(1)}, f32[128,576]{0,1:T(8,128)S(1)}, u32[]{:S(2)}, u32[]{:S(2)}) %collective-permute-start) | collective-permute-done | bytes 294944 | tf_op jit(solution)/shard_map/while/body/eval_jaxpr/ppermute | solution.py:13
  182.8 9.0 %collective-permute-done = f32[128,576]{0,1:T(8,128)S(1)} collective-permute-done((f32[128,576]{0,1:T(8,128)S(1)}, f32[128,576]{0,1:T(8,128)S(1)}, u32[]{:S(2)}, u32[]{:S(2)}) %collective-permute-start) | collective-permute-done | bytes 294944 | tf_op jit(solution)/shard_map/while/body/eval_jaxpr/ppermute | solution.py:13
  198.7 9.0 %collective-permute-done = f32[128,576]{0,1:T(8,128)S(1)} collective-permute-done((f32[128,576]{0,1:T(8,128)S(1)}, f32[128,576]{0,1:T(8,128)S(1)}, u32[]{:S(2)}, u32[]{:S(2)}) %collective-permute-start) | collective-permute-done | bytes 294944 | tf_op jit(solution)/shard_map/while/body/eval_jaxpr/ppermute | solution.py:13
  214.5 9.0 %collective-permute-done = f32[128,576]{0,1:T(8,128)S(1)} collective-permute-done((f32[128,576]{0,1:T(8,128)S(1)}, f32[128,576]{0,1:T(8,128)S(1)}, u32[]{:S(2)}, u32[]{:S(2)}) %collective-permute-start) | collective-permute-done | bytes 294944 | tf_op jit(solution)/shard_map/while/body/eval_jaxpr/ppermute | solution.py:13
  230.3 9.0 %collective-permute-done = f32[128,576]{0,1:T(8,128)S(1)} collective-permute-done((f32[128,576]{0,1:T(8,128)S(1)}, f32[128,576]{0,1:T(8,128)S(1)}, u32[]{:S(2)}, u32[]{:S(2)}) %collective-permute-start) | collective-permute-done | bytes 294944 | tf_op jit(solution)/shard_map/while/body/eval_jaxpr/ppermute | solution.py:13
  246.2 9.0 %collective-permute-done = f32[128,576]{0,1:T(8,128)S(1)} collective-permute-done((f32[128,576]{0,1:T(8,128)S(1)}, f32[128,576]{0,1:T(8,128)S(1)}, u32[]{:S(2)}, u32[]{:S(2)}) %collective-permute-start) | collective-permute-done | bytes 294944 | tf_op jit(solution)/shard_map/while/body/eval_jaxpr/ppermute | solution.py:13
  262.0 9.0 %collective-permute-done = f32[128,576]{0,1:T(8,128)S(1)} collective-permute-done((f32[128,576]{0,1:T(8,128)S(1)}, f32[128,576]{0,1:T(8,128)S(1)}, u32[]{:S(2)}, u32[]{:S(2)}) %collective-permute-start) | collective-permute-done | bytes 294944 | tf_op jit(solution)/shard_map/while/body/eval_jaxpr/ppermute | solution.py:13
  277.9 9.0 %collective-permute-done = f32[128,576]{0,1:T(8,128)S(1)} collective-permute-done((f32[128,576]{0,1:T(8,128)S(1)}, f32[128,576]{0,1:T(8,128)S(1)}, u32[]{:S(2)}, u32[]{:S(2)}) %collective-permute-start) | collective-permute-done | bytes 294944 | tf_op jit(solution)/shard_map/while/body/eval_jaxpr/ppermute | solution.py:13
  293.7 9.0 %collective-permute-done = f32[128,576]{0,1:T(8,128)S(1)} collective-permute-done((f32[128,576]{0,1:T(8,128)S(1)}, f32[128,576]{0,1:T(8,128)S(1)}, u32[]{:S(2)}, u32[]{:S(2)}) %collective-permute-start) | collective-permute-done | bytes 294944 | tf_op jit(solution)/shard_map/while/body/eval_jaxpr/ppermute | solution.py:13
  309.5 9.1 %collective-permute-done = f32[128,576]{0,1:T(8,128)S(1)} collective-permute-done((f32[128,576]{0,1:T(8,128)S(1)}, f32[128,576]{0,1:T(8,128)S(1)}, u32[]{:S(2)}, u32[]{:S(2)}) %collective-permute-start) | collective-permute-done | bytes 294944 | tf_op jit(solution)/shard_map/while/body/eval_jaxpr/ppermute | solution.py:13
  325.5 9.1 %collective-permute-done = f32[128,576]{0,1:T(8,128)S(1)} collective-permute-done((f32[128,576]{0,1:T(8,128)S(1)}, f32[128,576]{0,1:T(8,128)S(1)}, u32[]{:S(2)}, u32[]{:S(2)}) %collective-permute-start) | collective-permute-done | bytes 294944 | tf_op jit(solution)/shard_map/while/body/eval_jaxpr/ppermute | solution.py:13
  341.4 9.1 %collective-permute-done = f32[128,576]{0,1:T(8,128)S(1)} collective-permute-done((f32[128,576]{0,1:T(8,128)S(1)}, f32[128,576]{0,1:T(8,128)S(1)}, u32[]{:S(2)}, u32[]{:S(2)}) %collective-permute-start) | collective-permute-done | bytes 294944 | tf_op jit(solution)/shard_map/while/body/eval_jaxpr/ppermute | solution.py:13
  357.4 9.1 %collective-permute-done = f32[128,576]{0,1:T(8,128)S(1)} collective-permute-done((f32[128,576]{0,1:T(8,128)S(1)}, f32[128,576]{0,1:T(8,128)S(1)}, u32[]{:S(2)}, u32[]{:S(2)}) %collective-permute-start) | collective-permute-done | bytes 294944 | tf_op jit(solution)/shard_map/while/body/eval_jaxpr/ppermute | solution.py:13
  373.3 9.1 %collective-permute-done = f32[128,576]{0,1:T(8,128)S(1)} collective-permute-done((f32[128,576]{0,1:T(8,128)S(1)}, f32[128,576]{0,1:T(8,128)S(1)}, u32[]{:S(2)}, u32[]{:S(2)}) %collective-permute-start) | collective-permute-done | bytes 294944 | tf_op jit(solution)/shard_map/while/body/eval_jaxpr/ppermute | solution.py:13
  389.2 9.1 %collective-permute-done = f32[128,576]{0,1:T(8,128)S(1)} collective-permute-done((f32[128,576]{0,1:T(8,128)S(1)}, f32[128,576]{0,1:T(8,128)S(1)}, u32[]{:S(2)}, u32[]{:S(2)}) %collective-permute-start) | collective-permute-done | bytes 294944 | tf_op jit(solution)/shard_map/while/body/eval_jaxpr/ppermute | solution.py:13
  405.2 9.1 %collective-permute-done = f32[128,576]{0,1:T(8,128)S(1)} collective-permute-done((f32[128,576]{0,1:T(8,128)S(1)}, f32[128,576]{0,1:T(8,128)S(1)}, u32[]{:S(2)}, u32[]{:S(2)}) %collective-permute-start) | collective-permute-done | bytes 294944 | tf_op jit(solution)/shard_map/while/body/eval_jaxpr/ppermute | solution.py:13
  421.1 9.1 %collective-permute-done = f32[128,576]{0,1:T(8,128)S(1)} collective-permute-done((f32[128,576]{0,1:T(8,128)S(1)}, f32[128,576]{0,1:T(8,128)S(1)}, u32[]{:S(2)}, u32[]{:S(2)}) %collective-permute-start) | collective-permute-done | bytes 294944 | tf_op jit(solution)/shard_map/while/body/eval_jaxpr/ppermute | solution.py:13
  437.1 9.1 %collective-permute-done = f32[128,576]{0,1:T(8,128)S(1)} collective-permute-done((f32[128,576]{0,1:T(8,128)S(1)}, f32[128,576]{0,1:T(8,128)S(1)}, u32[]{:S(2)}, u32[]{:S(2)}) %collective-permute-start) | collective-permute-done | bytes 294944 | tf_op jit(solution)/shard_map/while/body/eval_jaxpr/ppermute | solution.py:13
  453.0 9.1 %collective-permute-done = f32[128,576]{0,1:T(8,128)S(1)} collective-permute-done((f32[128,576]{0,1:T(8,128)S(1)}, f32[128,576]{0,1:T(8,128)S(1)}, u32[]{:S(2)}, u32[]{:S(2)}) %collective-permute-start) | collective-permute-done | bytes 294944 | tf_op jit(solution)/shard_map/while/body/eval_jaxpr/ppermute | solution.py:13
  468.9 9.1 %collective-permute-done = f32[128,576]{0,1:T(8,128)S(1)} collective-permute-done((f32[128,576]{0,1:T(8,128)S(1)}, f32[128,576]{0,1:T(8,128)S(1)}, u32[]{:S(2)}, u32[]{:S(2)}) %collective-permute-start) | collective-permute-done | bytes 294944 | tf_op jit(solution)/shard_map/while/body/eval_jaxpr/ppermute | solution.py:13
  484.9 9.1 %collective-permute-done = f32[128,576]{0,1:T(8,128)S(1)} collective-permute-done((f32[128,576]{0,1:T(8,128)S(1)}, f32[128,576]{0,1:T(8,128)S(1)}, u32[]{:S(2)}, u32[]{:S(2)}) %collective-permute-start) | collective-permute-done | bytes 294944 | tf_op jit(solution)/shard_map/while/body/eval_jaxpr/ppermute | solution.py:13
  500.8 9.1 %collective-permute-done = f32[128,576]{0,1:T(8,128)S(1)} collective-permute-done((f32[128,576]{0,1:T(8,128)S(1)}, f32[128,576]{0,1:T(8,128)S(1)}, u32[]{:S(2)}, u32[]{:S(2)}) %collective-permute-start) | collective-permute-done | bytes 294944 | tf_op jit(solution)/shard_map/while/body/eval_jaxpr/ppermute | solution.py:13
  516.8 9.1 %collective-permute-done = f32[128,576]{0,1:T(8,128)S(1)} collective-permute-done((f32[128,576]{0,1:T(8,128)S(1)}, f32[128,576]{0,1:T(8,128)S(1)}, u32[]{:S(2)}, u32[]{:S(2)}) %collective-permute-start) | collective-permute-done | bytes 294944 | tf_op jit(solution)/shard_map/while/body/eval_jaxpr/ppermute | solution.py:13
  532.7 9.1 %collective-permute-done = f32[128,576]{0,1:T(8,128)S(1)} collective-permute-done((f32[128,576]{0,1:T(8,128)S(1)}, f32[128,576]{0,1:T(8,128)S(1)}, u32[]{:S(2)}, u32[]{:S(2)}) %collective-permute-start) | collective-permute-done | bytes 294944 | tf_op jit(solution)/shard_map/while/body/eval_jaxpr/ppermute | solution.py:13
  548.7 9.1 %collective-permute-done = f32[128,576]{0,1:T(8,128)S(1)} collective-permute-done((f32[128,576]{0,1:T(8,128)S(1)}, f32[128,576]{0,1:T(8,128)S(1)}, u32[]{:S(2)}, u32[]{:S(2)}) %collective-permute-start) | collective-permute-done | bytes 294944 | tf_op jit(solution)/shard_map/while/body/eval_jaxpr/ppermute | solution.py:13
  564.6 9.1 %collective-permute-done = f32[128,576]{0,1:T(8,128)S(1)} collective-permute-done((f32[128,576]{0,1:T(8,128)S(1)}, f32[128,576]{0,1:T(8,128)S(1)}, u32[]{:S(2)}, u32[]{:S(2)}) %collective-permute-start) | collective-permute-done | bytes 294944 | tf_op jit(solution)/shard_map/while/body/eval_jaxpr/ppermute | solution.py:13
  580.1 149.8 %all-reduce.5.cloned.1.call-done = f32[128,576]{1,0:T(8,128)} async-done(((f32[128,576]{1,0:T(8,128)}), f32[128,576]{1,0:T(8,128)}) %all-reduce.5.cloned.1.call-update) | async-done | bytes 294928
  (281 shorter events, 235.8 us)
Async XLA Ops:
  7.2 79.9 %all-gather.2.cloned.1.call-start = ((), (), s32[]{:S(2)}) async-start(), calls=%async_computation | async-start | bytes 5406720 | tf_op jit(solution)/shard_map/all_gather | solution.py:81
  8.9 720.9 %all-reduce.5.cloned.1.call-start = ((), (), s32[]{:S(2)}) async-start(), calls=%async_computation.1 | async-start | bytes 655360
  97.6 8.0 %collective-permute-start = (f32[128,576]{0,1:T(8,128)S(1)}, f32[128,576]{0,1:T(8,128)S(1)}, u32[]{:S(2)}, u32[]{:S(2)}) collective-permute-start(f32[128,576]{0,1:T(8,128)S(1)} %fusion.95), channel_id=1, source_target_pairs={{496,0},{0,16},{16,32},{32,48},{48,64},{64,80},{80,96},{96,112},{1... | collective-permute-start | bytes 884744 | tf_op jit(solution)/shard_map/while/body/eval_jaxpr/ppermute | solution.py:13
  109.2 8.0 %collective-permute-start = (f32[128,576]{0,1:T(8,128)S(1)}, f32[128,576]{0,1:T(8,128)S(1)}, u32[]{:S(2)}, u32[]{:S(2)}) collective-permute-start(f32[128,576]{0,1:T(8,128)S(1)} %fusion.95), channel_id=1, source_target_pairs={{496,0},{0,16},{16,32},{32,48},{48,64},{64,80},{80,96},{96,112},{1... | collective-permute-start | bytes 884744 | tf_op jit(solution)/shard_map/while/body/eval_jaxpr/ppermute | solution.py:13
  132.5 11.8 %collective-permute-start = (f32[128,576]{0,1:T(8,128)S(1)}, f32[128,576]{0,1:T(8,128)S(1)}, u32[]{:S(2)}, u32[]{:S(2)}) collective-permute-start(f32[128,576]{0,1:T(8,128)S(1)} %fusion.95), channel_id=1, source_target_pairs={{496,0},{0,16},{16,32},{32,48},{48,64},{64,80},{80,96},{96,112},{1... | collective-permute-start | bytes 884744 | tf_op jit(solution)/shard_map/while/body/eval_jaxpr/ppermute | solution.py:13
  147.9 12.3 %collective-permute-start = (f32[128,576]{0,1:T(8,128)S(1)}, f32[128,576]{0,1:T(8,128)S(1)}, u32[]{:S(2)}, u32[]{:S(2)}) collective-permute-start(f32[128,576]{0,1:T(8,128)S(1)} %fusion.95), channel_id=1, source_target_pairs={{496,0},{0,16},{16,32},{32,48},{48,64},{64,80},{80,96},{96,112},{1... | collective-permute-start | bytes 884744 | tf_op jit(solution)/shard_map/while/body/eval_jaxpr/ppermute | solution.py:13
  163.7 12.3 %collective-permute-start = (f32[128,576]{0,1:T(8,128)S(1)}, f32[128,576]{0,1:T(8,128)S(1)}, u32[]{:S(2)}, u32[]{:S(2)}) collective-permute-start(f32[128,576]{0,1:T(8,128)S(1)} %fusion.95), channel_id=1, source_target_pairs={{496,0},{0,16},{16,32},{32,48},{48,64},{64,80},{80,96},{96,112},{1... | collective-permute-start | bytes 884744 | tf_op jit(solution)/shard_map/while/body/eval_jaxpr/ppermute | solution.py:13
  179.6 12.3 %collective-permute-start = (f32[128,576]{0,1:T(8,128)S(1)}, f32[128,576]{0,1:T(8,128)S(1)}, u32[]{:S(2)}, u32[]{:S(2)}) collective-permute-start(f32[128,576]{0,1:T(8,128)S(1)} %fusion.95), channel_id=1, source_target_pairs={{496,0},{0,16},{16,32},{32,48},{48,64},{64,80},{80,96},{96,112},{1... | collective-permute-start | bytes 884744 | tf_op jit(solution)/shard_map/while/body/eval_jaxpr/ppermute | solution.py:13
  195.4 12.3 %collective-permute-start = (f32[128,576]{0,1:T(8,128)S(1)}, f32[128,576]{0,1:T(8,128)S(1)}, u32[]{:S(2)}, u32[]{:S(2)}) collective-permute-start(f32[128,576]{0,1:T(8,128)S(1)} %fusion.95), channel_id=1, source_target_pairs={{496,0},{0,16},{16,32},{32,48},{48,64},{64,80},{80,96},{96,112},{1... | collective-permute-start | bytes 884744 | tf_op jit(solution)/shard_map/while/body/eval_jaxpr/ppermute | solution.py:13
  211.3 12.3 %collective-permute-start = (f32[128,576]{0,1:T(8,128)S(1)}, f32[128,576]{0,1:T(8,128)S(1)}, u32[]{:S(2)}, u32[]{:S(2)}) collective-permute-start(f32[128,576]{0,1:T(8,128)S(1)} %fusion.95), channel_id=1, source_target_pairs={{496,0},{0,16},{16,32},{32,48},{48,64},{64,80},{80,96},{96,112},{1... | collective-permute-start | bytes 884744 | tf_op jit(solution)/shard_map/while/body/eval_jaxpr/ppermute | solution.py:13
  227.1 12.3 %collective-permute-start = (f32[128,576]{0,1:T(8,128)S(1)}, f32[128,576]{0,1:T(8,128)S(1)}, u32[]{:S(2)}, u32[]{:S(2)}) collective-permute-start(f32[128,576]{0,1:T(8,128)S(1)} %fusion.95), channel_id=1, source_target_pairs={{496,0},{0,16},{16,32},{32,48},{48,64},{64,80},{80,96},{96,112},{1... | collective-permute-start | bytes 884744 | tf_op jit(solution)/shard_map/while/body/eval_jaxpr/ppermute | solution.py:13
  243.0 12.3 %collective-permute-start = (f32[128,576]{0,1:T(8,128)S(1)}, f32[128,576]{0,1:T(8,128)S(1)}, u32[]{:S(2)}, u32[]{:S(2)}) collective-permute-start(f32[128,576]{0,1:T(8,128)S(1)} %fusion.95), channel_id=1, source_target_pairs={{496,0},{0,16},{16,32},{32,48},{48,64},{64,80},{80,96},{96,112},{1... | collective-permute-start | bytes 884744 | tf_op jit(solution)/shard_map/while/body/eval_jaxpr/ppermute | solution.py:13
  258.8 12.3 %collective-permute-start = (f32[128,576]{0,1:T(8,128)S(1)}, f32[128,576]{0,1:T(8,128)S(1)}, u32[]{:S(2)}, u32[]{:S(2)}) collective-permute-start(f32[128,576]{0,1:T(8,128)S(1)} %fusion.95), channel_id=1, source_target_pairs={{496,0},{0,16},{16,32},{32,48},{48,64},{64,80},{80,96},{96,112},{1... | collective-permute-start | bytes 884744 | tf_op jit(solution)/shard_map/while/body/eval_jaxpr/ppermute | solution.py:13
  274.6 12.3 %collective-permute-start = (f32[128,576]{0,1:T(8,128)S(1)}, f32[128,576]{0,1:T(8,128)S(1)}, u32[]{:S(2)}, u32[]{:S(2)}) collective-permute-start(f32[128,576]{0,1:T(8,128)S(1)} %fusion.95), channel_id=1, source_target_pairs={{496,0},{0,16},{16,32},{32,48},{48,64},{64,80},{80,96},{96,112},{1... | collective-permute-start | bytes 884744 | tf_op jit(solution)/shard_map/while/body/eval_jaxpr/ppermute | solution.py:13
  290.5 12.3 %collective-permute-start = (f32[128,576]{0,1:T(8,128)S(1)}, f32[128,576]{0,1:T(8,128)S(1)}, u32[]{:S(2)}, u32[]{:S(2)}) collective-permute-start(f32[128,576]{0,1:T(8,128)S(1)} %fusion.95), channel_id=1, source_target_pairs={{496,0},{0,16},{16,32},{32,48},{48,64},{64,80},{80,96},{96,112},{1... | collective-permute-start | bytes 884744 | tf_op jit(solution)/shard_map/while/body/eval_jaxpr/ppermute | solution.py:13
  306.3 12.3 %collective-permute-start = (f32[128,576]{0,1:T(8,128)S(1)}, f32[128,576]{0,1:T(8,128)S(1)}, u32[]{:S(2)}, u32[]{:S(2)}) collective-permute-start(f32[128,576]{0,1:T(8,128)S(1)} %fusion.95), channel_id=1, source_target_pairs={{496,0},{0,16},{16,32},{32,48},{48,64},{64,80},{80,96},{96,112},{1... | collective-permute-start | bytes 884744 | tf_op jit(solution)/shard_map/while/body/eval_jaxpr/ppermute | solution.py:13
  322.3 12.4 %collective-permute-start = (f32[128,576]{0,1:T(8,128)S(1)}, f32[128,576]{0,1:T(8,128)S(1)}, u32[]{:S(2)}, u32[]{:S(2)}) collective-permute-start(f32[128,576]{0,1:T(8,128)S(1)} %fusion.95), channel_id=1, source_target_pairs={{496,0},{0,16},{16,32},{32,48},{48,64},{64,80},{80,96},{96,112},{1... | collective-permute-start | bytes 884744 | tf_op jit(solution)/shard_map/while/body/eval_jaxpr/ppermute | solution.py:13
  338.2 12.4 %collective-permute-start = (f32[128,576]{0,1:T(8,128)S(1)}, f32[128,576]{0,1:T(8,128)S(1)}, u32[]{:S(2)}, u32[]{:S(2)}) collective-permute-start(f32[128,576]{0,1:T(8,128)S(1)} %fusion.95), channel_id=1, source_target_pairs={{496,0},{0,16},{16,32},{32,48},{48,64},{64,80},{80,96},{96,112},{1... | collective-permute-start | bytes 884744 | tf_op jit(solution)/shard_map/while/body/eval_jaxpr/ppermute | solution.py:13
  354.1 12.4 %collective-permute-start = (f32[128,576]{0,1:T(8,128)S(1)}, f32[128,576]{0,1:T(8,128)S(1)}, u32[]{:S(2)}, u32[]{:S(2)}) collective-permute-start(f32[128,576]{0,1:T(8,128)S(1)} %fusion.95), channel_id=1, source_target_pairs={{496,0},{0,16},{16,32},{32,48},{48,64},{64,80},{80,96},{96,112},{1... | collective-permute-start | bytes 884744 | tf_op jit(solution)/shard_map/while/body/eval_jaxpr/ppermute | solution.py:13
  370.1 12.4 %collective-permute-start = (f32[128,576]{0,1:T(8,128)S(1)}, f32[128,576]{0,1:T(8,128)S(1)}, u32[]{:S(2)}, u32[]{:S(2)}) collective-permute-start(f32[128,576]{0,1:T(8,128)S(1)} %fusion.95), channel_id=1, source_target_pairs={{496,0},{0,16},{16,32},{32,48},{48,64},{64,80},{80,96},{96,112},{1... | collective-permute-start | bytes 884744 | tf_op jit(solution)/shard_map/while/body/eval_jaxpr/ppermute | solution.py:13
  386.0 12.4 %collective-permute-start = (f32[128,576]{0,1:T(8,128)S(1)}, f32[128,576]{0,1:T(8,128)S(1)}, u32[]{:S(2)}, u32[]{:S(2)}) collective-permute-start(f32[128,576]{0,1:T(8,128)S(1)} %fusion.95), channel_id=1, source_target_pairs={{496,0},{0,16},{16,32},{32,48},{48,64},{64,80},{80,96},{96,112},{1... | collective-permute-start | bytes 884744 | tf_op jit(solution)/shard_map/while/body/eval_jaxpr/ppermute | solution.py:13
  402.0 12.4 %collective-permute-start = (f32[128,576]{0,1:T(8,128)S(1)}, f32[128,576]{0,1:T(8,128)S(1)}, u32[]{:S(2)}, u32[]{:S(2)}) collective-permute-start(f32[128,576]{0,1:T(8,128)S(1)} %fusion.95), channel_id=1, source_target_pairs={{496,0},{0,16},{16,32},{32,48},{48,64},{64,80},{80,96},{96,112},{1... | collective-permute-start | bytes 884744 | tf_op jit(solution)/shard_map/while/body/eval_jaxpr/ppermute | solution.py:13
  417.9 12.4 %collective-permute-start = (f32[128,576]{0,1:T(8,128)S(1)}, f32[128,576]{0,1:T(8,128)S(1)}, u32[]{:S(2)}, u32[]{:S(2)}) collective-permute-start(f32[128,576]{0,1:T(8,128)S(1)} %fusion.95), channel_id=1, source_target_pairs={{496,0},{0,16},{16,32},{32,48},{48,64},{64,80},{80,96},{96,112},{1... | collective-permute-start | bytes 884744 | tf_op jit(solution)/shard_map/while/body/eval_jaxpr/ppermute | solution.py:13
  433.8 12.4 %collective-permute-start = (f32[128,576]{0,1:T(8,128)S(1)}, f32[128,576]{0,1:T(8,128)S(1)}, u32[]{:S(2)}, u32[]{:S(2)}) collective-permute-start(f32[128,576]{0,1:T(8,128)S(1)} %fusion.95), channel_id=1, source_target_pairs={{496,0},{0,16},{16,32},{32,48},{48,64},{64,80},{80,96},{96,112},{1... | collective-permute-start | bytes 884744 | tf_op jit(solution)/shard_map/while/body/eval_jaxpr/ppermute | solution.py:13
  449.8 12.4 %collective-permute-start = (f32[128,576]{0,1:T(8,128)S(1)}, f32[128,576]{0,1:T(8,128)S(1)}, u32[]{:S(2)}, u32[]{:S(2)}) collective-permute-start(f32[128,576]{0,1:T(8,128)S(1)} %fusion.95), channel_id=1, source_target_pairs={{496,0},{0,16},{16,32},{32,48},{48,64},{64,80},{80,96},{96,112},{1... | collective-permute-start | bytes 884744 | tf_op jit(solution)/shard_map/while/body/eval_jaxpr/ppermute | solution.py:13
  465.7 12.4 %collective-permute-start = (f32[128,576]{0,1:T(8,128)S(1)}, f32[128,576]{0,1:T(8,128)S(1)}, u32[]{:S(2)}, u32[]{:S(2)}) collective-permute-start(f32[128,576]{0,1:T(8,128)S(1)} %fusion.95), channel_id=1, source_target_pairs={{496,0},{0,16},{16,32},{32,48},{48,64},{64,80},{80,96},{96,112},{1... | collective-permute-start | bytes 884744 | tf_op jit(solution)/shard_map/while/body/eval_jaxpr/ppermute | solution.py:13
  481.7 12.4 %collective-permute-start = (f32[128,576]{0,1:T(8,128)S(1)}, f32[128,576]{0,1:T(8,128)S(1)}, u32[]{:S(2)}, u32[]{:S(2)}) collective-permute-start(f32[128,576]{0,1:T(8,128)S(1)} %fusion.95), channel_id=1, source_target_pairs={{496,0},{0,16},{16,32},{32,48},{48,64},{64,80},{80,96},{96,112},{1... | collective-permute-start | bytes 884744 | tf_op jit(solution)/shard_map/while/body/eval_jaxpr/ppermute | solution.py:13
  497.6 12.4 %collective-permute-start = (f32[128,576]{0,1:T(8,128)S(1)}, f32[128,576]{0,1:T(8,128)S(1)}, u32[]{:S(2)}, u32[]{:S(2)}) collective-permute-start(f32[128,576]{0,1:T(8,128)S(1)} %fusion.95), channel_id=1, source_target_pairs={{496,0},{0,16},{16,32},{32,48},{48,64},{64,80},{80,96},{96,112},{1... | collective-permute-start | bytes 884744 | tf_op jit(solution)/shard_map/while/body/eval_jaxpr/ppermute | solution.py:13
  513.6 12.4 %collective-permute-start = (f32[128,576]{0,1:T(8,128)S(1)}, f32[128,576]{0,1:T(8,128)S(1)}, u32[]{:S(2)}, u32[]{:S(2)}) collective-permute-start(f32[128,576]{0,1:T(8,128)S(1)} %fusion.95), channel_id=1, source_target_pairs={{496,0},{0,16},{16,32},{32,48},{48,64},{64,80},{80,96},{96,112},{1... | collective-permute-start | bytes 884744 | tf_op jit(solution)/shard_map/while/body/eval_jaxpr/ppermute | solution.py:13
  529.5 12.4 %collective-permute-start = (f32[128,576]{0,1:T(8,128)S(1)}, f32[128,576]{0,1:T(8,128)S(1)}, u32[]{:S(2)}, u32[]{:S(2)}) collective-permute-start(f32[128,576]{0,1:T(8,128)S(1)} %fusion.95), channel_id=1, source_target_pairs={{496,0},{0,16},{16,32},{32,48},{48,64},{64,80},{80,96},{96,112},{1... | collective-permute-start | bytes 884744 | tf_op jit(solution)/shard_map/while/body/eval_jaxpr/ppermute | solution.py:13
  545.4 12.4 %collective-permute-start = (f32[128,576]{0,1:T(8,128)S(1)}, f32[128,576]{0,1:T(8,128)S(1)}, u32[]{:S(2)}, u32[]{:S(2)}) collective-permute-start(f32[128,576]{0,1:T(8,128)S(1)} %fusion.95), channel_id=1, source_target_pairs={{496,0},{0,16},{16,32},{32,48},{48,64},{64,80},{80,96},{96,112},{1... | collective-permute-start | bytes 884744 | tf_op jit(solution)/shard_map/while/body/eval_jaxpr/ppermute | solution.py:13
  561.4 12.4 %collective-permute-start = (f32[128,576]{0,1:T(8,128)S(1)}, f32[128,576]{0,1:T(8,128)S(1)}, u32[]{:S(2)}, u32[]{:S(2)}) collective-permute-start(f32[128,576]{0,1:T(8,128)S(1)} %fusion.95), channel_id=1, source_target_pairs={{496,0},{0,16},{16,32},{32,48},{48,64},{64,80},{80,96},{96,112},{1... | collective-permute-start | bytes 884744 | tf_op jit(solution)/shard_map/while/body/eval_jaxpr/ppermute | solution.py:13
  (4 other events, 253.5 us)
Sparse Core Ops, SparseCore 0:
  11.7 75.2 all-gather.1
  576.1 153.7 all-reduce.4
where the time goes:
time: 741 us; the launch traced here: 738 us
  waiting for transfers between devices  494 us (67%)
  matrix products  138 us (19%)
  starting transfers between devices  59.9 us (8%)
  other arithmetic  22.5 us (3%)
  between operations  15.5 us (2%)
    ppermute x31, waiting for transfers between devices, shifted(): return lax.ppermute(block, axis, route)  269 us
    unnamed x3, waiting for transfers between devices  150 us
    all_gather x1, waiting for transfers between devices, per_device(): block_rows = lax.all_gather(latents, 'seq', axis=0, tiled=True)  75.9 us
    ppermute x31, starting transfers between devices, shifted(): return lax.ppermute(block, axis, route)  59.8 us
    dot_general x33, matrix products, score_block(): lax.dot_general(block_rows, query_rows, (((1,), (1,)), ((), ())), preferr...  42.6 us
    dot_general x32, matrix products, grad_block(): lax.dot_general(dscore, block_rows, (((0,), (0,)), ((), ())), preferred_e...  40.9 us
    dot_general x32, matrix products, grad_block(): lax.dot_general(block_rows[:, :value_width], grad_rows, (((1,), (1,)), ((...  36.5 us
    add x32, other arithmetic, per_device(): query_pos = query_start[0] + lax.iota(jnp.int32, row_count) // head_count  20.1 us
  transfers between devices with their start and end apart: 33, of which 33 were waited for; matrix products, arithmetic and copies ran while one was open for 6% of the time, Pallas kernels for 0%

commit v1 on v0

--- a/solution.py
+++ b/solution.py
@@ -78,7 +78,8 @@
         jnp.full((row_count,), masked_score, jnp.float32),
         jnp.zeros((row_count,), jnp.float32),
     )
-    block_rows = lax.all_gather(latents, "seq", axis=0, tiled=True)
+    outgoing = jnp.stack([latents] * lax.axis_size("seq"))
+    block_rows = jnp.concatenate(lax.all_to_all(outgoing, "seq", 0, 0), axis=0)
     running = start_state
     running = norm_step(running, block_rows, jnp.int32(0), query_rows, query_pos)
     add_stored = block_rows

time: 741 us -> 790 us (1.066)
  waiting for transfers between devices: 494 us -> 528 us
  starting transfers between devices: 59.9 us -> 73.2 us
    all_to_all x0 -> x1, waiting for transfers between devices: none -> 107 us  [per_device(): block_rows = jnp.concatenate(lax.all_to_all(outgoing, 'seq', 0, 0), axis=0)]
    all_gather x1 -> x0, waiting for transfers between devices: 75.9 us -> none  [per_device(): block_rows = lax.all_gather(latents, 'seq', axis=0, tiled=True)]
    all_to_all x0 -> x1, starting transfers between devices: none -> 13.6 us  [per_device(): block_rows = jnp.concatenate(lax.all_to_all(outgoing, 'seq', 0, 0), axis=0)]
    unnamed x3 -> x2, waiting for transfers between devices: 150 us -> 147 us
  transfers between devices with their start and end apart: 33 -> 33, of which waited for: 33 -> 33; matrix products, arithmetic and copies ran while one was open for 6% -> 5% of each run, Pallas kernels for 0% -> 0%
where the time goes in v1:
time: 790 us; the launch traced here: 786 us
  waiting for transfers between devices  528 us (67%)
  matrix products  134 us (17%)
  starting transfers between devices  73.2 us (9%)
  other arithmetic  21.4 us (3%)
  between operations  15.5 us (2%)
  local copies, waits for them, and re-layouts  12.4 us (2%)
    ppermute x31, waiting for transfers between devices, shifted(): return lax.ppermute(block, axis, route)  274 us
    unnamed x2, waiting for transfers between devices  147 us
    all_to_all x1, waiting for transfers between devices, per_device(): block_rows = jnp.concatenate(lax.all_to_all(outgoing, 'seq', 0, 0), axis=0)  107 us
    ppermute x31, starting transfers between devices, shifted(): return lax.ppermute(block, axis, route)  59.5 us
    dot_general x33, matrix products, score_block(): lax.dot_general(block_rows, query_rows, (((1,), (1,)), ((), ())), preferr...  41.4 us
    dot_general x32, matrix products, grad_block(): lax.dot_general(dscore, block_rows, (((0,), (0,)), ((), ())), preferred_e...  38.5 us
    dot_general x32, matrix products, grad_block(): lax.dot_general(block_rows[:, :value_width], grad_rows, (((1,), (1,)), ((...  35.8 us
    add x32, other arithmetic, per_device(): query_pos = query_start[0] + lax.iota(jnp.int32, row_count) // head_count  20.1 us
  transfers between devices with their start and end apart: 33, of which 33 were waited for; matrix products, arithmetic and copies ran while one was open for 5% of the time, Pallas kernels for 0%

profile of v1, /device:TPU:2, one launch (start us, length us, event | category | flops | bytes accessed | tf_op | source)
XLA Modules:
  0.0 786.4 jit_solution(217087963814648242)
XLA Ops:
  11.3 13.6 %all-to-all-start = ((bf16[32,128,576]{1,2,0:T(8,128)(2,1)}), bf16[32,128,576]{1,2,0:T(8,128)(2,1)}, u32[]{:S(2)}, u32[]{:S(2)}) async-start(bf16[32,128,576]{1,2,0:T(8,128)(2,1)} %stack.2), calls=%async_computation | async-start | bytes 9437184 | tf_op jit(solution)/shard_map/all_to_all | solution.py:82
  26.0 106.9 %all-to-all-done = bf16[32,128,576]{1,2,0:T(8,128)(2,1)} async-done(((bf16[32,128,576]{1,2,0:T(8,128)(2,1)}), bf16[32,128,576]{1,2,0:T(8,128)(2,1)}, u32[]{:S(2)}, u32[]{:S(2)}) %all-to-all-start) | async-done | bytes 4718624 | tf_op jit(solution)/shard_map/all_to_all | solution.py:82
  143.5 482.2 %while.19 = (s32[]{:T(128)}, f32[128,576]{0,1:T(8,128)S(1)}, f32[256,576]{0,1:T(8,128)S(1)}, s32[]{:T(128)}, bf16[4096,576]{0,1:T(8,128)(2,1)}, /*index=5*/bf16[...) while((s32[]{:T(128)}, f32[128,576]{0,1:T(8,128)S(1)}, ...), condition=%wide.wide.region_4.5_spmd.clone, body=%wide.wide.region_3.4_spmd.clone.sunk | while | flops 181127568 | bytes 5608862 | solution.py:105
  185.8 10.5 %collective-permute-done = f32[128,576]{0,1:T(8,128)S(1)} collective-permute-done((f32[128,576]{0,1:T(8,128)S(1)}, f32[128,576]{0,1:T(8,128)S(1)}, u32[]{:S(2)}, u32[]{:S(2)}) %collective-permute-start) | collective-permute-done | bytes 294944 | tf_op jit(solution)/shard_map/while/body/eval_jaxpr/ppermute | solution.py:13
  203.1 9.1 %collective-permute-done = f32[128,576]{0,1:T(8,128)S(1)} collective-permute-done((f32[128,576]{0,1:T(8,128)S(1)}, f32[128,576]{0,1:T(8,128)S(1)}, u32[]{:S(2)}, u32[]{:S(2)}) %collective-permute-start) | collective-permute-done | bytes 294944 | tf_op jit(solution)/shard_map/while/body/eval_jaxpr/ppermute | solution.py:13
  219.0 9.1 %collective-permute-done = f32[128,576]{0,1:T(8,128)S(1)} collective-permute-done((f32[128,576]{0,1:T(8,128)S(1)}, f32[128,576]{0,1:T(8,128)S(1)}, u32[]{:S(2)}, u32[]{:S(2)}) %collective-permute-start) | collective-permute-done | bytes 294944 | tf_op jit(solution)/shard_map/while/body/eval_jaxpr/ppermute | solution.py:13
  234.8 9.1 %collective-permute-done = f32[128,576]{0,1:T(8,128)S(1)} collective-permute-done((f32[128,576]{0,1:T(8,128)S(1)}, f32[128,576]{0,1:T(8,128)S(1)}, u32[]{:S(2)}, u32[]{:S(2)}) %collective-permute-start) | collective-permute-done | bytes 294944 | tf_op jit(solution)/shard_map/while/body/eval_jaxpr/ppermute | solution.py:13
  250.7 9.1 %collective-permute-done = f32[128,576]{0,1:T(8,128)S(1)} collective-permute-done((f32[128,576]{0,1:T(8,128)S(1)}, f32[128,576]{0,1:T(8,128)S(1)}, u32[]{:S(2)}, u32[]{:S(2)}) %collective-permute-start) | collective-permute-done | bytes 294944 | tf_op jit(solution)/shard_map/while/body/eval_jaxpr/ppermute | solution.py:13
  266.5 9.1 %collective-permute-done = f32[128,576]{0,1:T(8,128)S(1)} collective-permute-done((f32[128,576]{0,1:T(8,128)S(1)}, f32[128,576]{0,1:T(8,128)S(1)}, u32[]{:S(2)}, u32[]{:S(2)}) %collective-permute-start) | collective-permute-done | bytes 294944 | tf_op jit(solution)/shard_map/while/body/eval_jaxpr/ppermute | solution.py:13
  282.4 9.1 %collective-permute-done = f32[128,576]{0,1:T(8,128)S(1)} collective-permute-done((f32[128,576]{0,1:T(8,128)S(1)}, f32[128,576]{0,1:T(8,128)S(1)}, u32[]{:S(2)}, u32[]{:S(2)}) %collective-permute-start) | collective-permute-done | bytes 294944 | tf_op jit(solution)/shard_map/while/body/eval_jaxpr/ppermute | solution.py:13
  298.2 9.1 %collective-permute-done = f32[128,576]{0,1:T(8,128)S(1)} collective-permute-done((f32[128,576]{0,1:T(8,128)S(1)}, f32[128,576]{0,1:T(8,128)S(1)}, u32[]{:S(2)}, u32[]{:S(2)}) %collective-permute-start) | collective-permute-done | bytes 294944 | tf_op jit(solution)/shard_map/while/body/eval_jaxpr/ppermute | solution.py:13
  314.0 9.1 %collective-permute-done = f32[128,576]{0,1:T(8,128)S(1)} collective-permute-done((f32[128,576]{0,1:T(8,128)S(1)}, f32[128,576]{0,1:T(8,128)S(1)}, u32[]{:S(2)}, u32[]{:S(2)}) %collective-permute-start) | collective-permute-done | bytes 294944 | tf_op jit(solution)/shard_map/while/body/eval_jaxpr/ppermute | solution.py:13
  329.9 9.1 %collective-permute-done = f32[128,576]{0,1:T(8,128)S(1)} collective-permute-done((f32[128,576]{0,1:T(8,128)S(1)}, f32[128,576]{0,1:T(8,128)S(1)}, u32[]{:S(2)}, u32[]{:S(2)}) %collective-permute-start) | collective-permute-done | bytes 294944 | tf_op jit(solution)/shard_map/while/body/eval_jaxpr/ppermute | solution.py:13
  345.7 9.1 %collective-permute-done = f32[128,576]{0,1:T(8,128)S(1)} collective-permute-done((f32[128,576]{0,1:T(8,128)S(1)}, f32[128,576]{0,1:T(8,128)S(1)}, u32[]{:S(2)}, u32[]{:S(2)}) %collective-permute-start) | collective-permute-done | bytes 294944 | tf_op jit(solution)/shard_map/while/body/eval_jaxpr/ppermute | solution.py:13
  361.6 9.1 %collective-permute-done = f32[128,576]{0,1:T(8,128)S(1)} collective-permute-done((f32[128,576]{0,1:T(8,128)S(1)}, f32[128,576]{0,1:T(8,128)S(1)}, u32[]{:S(2)}, u32[]{:S(2)}) %collective-permute-start) | collective-permute-done | bytes 294944 | tf_op jit(solution)/shard_map/while/body/eval_jaxpr/ppermute | solution.py:13
  377.4 9.1 %collective-permute-done = f32[128,576]{0,1:T(8,128)S(1)} collective-permute-done((f32[128,576]{0,1:T(8,128)S(1)}, f32[128,576]{0,1:T(8,128)S(1)}, u32[]{:S(2)}, u32[]{:S(2)}) %collective-permute-start) | collective-permute-done | bytes 294944 | tf_op jit(solution)/shard_map/while/body/eval_jaxpr/ppermute | solution.py:13
  393.3 9.2 %collective-permute-done = f32[128,576]{0,1:T(8,128)S(1)} collective-permute-done((f32[128,576]{0,1:T(8,128)S(1)}, f32[128,576]{0,1:T(8,128)S(1)}, u32[]{:S(2)}, u32[]{:S(2)}) %collective-permute-start) | collective-permute-done | bytes 294944 | tf_op jit(solution)/shard_map/while/body/eval_jaxpr/ppermute | solution.py:13
  409.2 9.2 %collective-permute-done = f32[128,576]{0,1:T(8,128)S(1)} collective-permute-done((f32[128,576]{0,1:T(8,128)S(1)}, f32[128,576]{0,1:T(8,128)S(1)}, u32[]{:S(2)}, u32[]{:S(2)}) %collective-permute-start) | collective-permute-done | bytes 294944 | tf_op jit(solution)/shard_map/while/body/eval_jaxpr/ppermute | solution.py:13
  425.1 9.2 %collective-permute-done = f32[128,576]{0,1:T(8,128)S(1)} collective-permute-done((f32[128,576]{0,1:T(8,128)S(1)}, f32[128,576]{0,1:T(8,128)S(1)}, u32[]{:S(2)}, u32[]{:S(2)}) %collective-permute-start) | collective-permute-done | bytes 294944 | tf_op jit(solution)/shard_map/while/body/eval_jaxpr/ppermute | solution.py:13
  441.1 9.2 %collective-permute-done = f32[128,576]{0,1:T(8,128)S(1)} collective-permute-done((f32[128,576]{0,1:T(8,128)S(1)}, f32[128,576]{0,1:T(8,128)S(1)}, u32[]{:S(2)}, u32[]{:S(2)}) %collective-permute-start) | collective-permute-done | bytes 294944 | tf_op jit(solution)/shard_map/while/body/eval_jaxpr/ppermute | solution.py:13
  457.0 9.2 %collective-permute-done = f32[128,576]{0,1:T(8,128)S(1)} collective-permute-done((f32[128,576]{0,1:T(8,128)S(1)}, f32[128,576]{0,1:T(8,128)S(1)}, u32[]{:S(2)}, u32[]{:S(2)}) %collective-permute-start) | collective-permute-done | bytes 294944 | tf_op jit(solution)/shard_map/while/body/eval_jaxpr/ppermute | solution.py:13
  473.0 9.2 %collective-permute-done = f32[128,576]{0,1:T(8,128)S(1)} collective-permute-done((f32[128,576]{0,1:T(8,128)S(1)}, f32[128,576]{0,1:T(8,128)S(1)}, u32[]{:S(2)}, u32[]{:S(2)}) %collective-permute-start) | collective-permute-done | bytes 294944 | tf_op jit(solution)/shard_map/while/body/eval_jaxpr/ppermute | solution.py:13
  488.9 9.2 %collective-permute-done = f32[128,576]{0,1:T(8,128)S(1)} collective-permute-done((f32[128,576]{0,1:T(8,128)S(1)}, f32[128,576]{0,1:T(8,128)S(1)}, u32[]{:S(2)}, u32[]{:S(2)}) %collective-permute-start) | collective-permute-done | bytes 294944 | tf_op jit(solution)/shard_map/while/body/eval_jaxpr/ppermute | solution.py:13
  504.9 9.2 %collective-permute-done = f32[128,576]{0,1:T(8,128)S(1)} collective-permute-done((f32[128,576]{0,1:T(8,128)S(1)}, f32[128,576]{0,1:T(8,128)S(1)}, u32[]{:S(2)}, u32[]{:S(2)}) %collective-permute-start) | collective-permute-done | bytes 294944 | tf_op jit(solution)/shard_map/while/body/eval_jaxpr/ppermute | solution.py:13
  520.8 9.2 %collective-permute-done = f32[128,576]{0,1:T(8,128)S(1)} collective-permute-done((f32[128,576]{0,1:T(8,128)S(1)}, f32[128,576]{0,1:T(8,128)S(1)}, u32[]{:S(2)}, u32[]{:S(2)}) %collective-permute-start) | collective-permute-done | bytes 294944 | tf_op jit(solution)/shard_map/while/body/eval_jaxpr/ppermute | solution.py:13
  536.7 9.2 %collective-permute-done = f32[128,576]{0,1:T(8,128)S(1)} collective-permute-done((f32[128,576]{0,1:T(8,128)S(1)}, f32[128,576]{0,1:T(8,128)S(1)}, u32[]{:S(2)}, u32[]{:S(2)}) %collective-permute-start) | collective-permute-done | bytes 294944 | tf_op jit(solution)/shard_map/while/body/eval_jaxpr/ppermute | solution.py:13
  552.7 9.2 %collective-permute-done = f32[128,576]{0,1:T(8,128)S(1)} collective-permute-done((f32[128,576]{0,1:T(8,128)S(1)}, f32[128,576]{0,1:T(8,128)S(1)}, u32[]{:S(2)}, u32[]{:S(2)}) %collective-permute-start) | collective-permute-done | bytes 294944 | tf_op jit(solution)/shard_map/while/body/eval_jaxpr/ppermute | solution.py:13
  568.6 9.2 %collective-permute-done = f32[128,576]{0,1:T(8,128)S(1)} collective-permute-done((f32[128,576]{0,1:T(8,128)S(1)}, f32[128,576]{0,1:T(8,128)S(1)}, u32[]{:S(2)}, u32[]{:S(2)}) %collective-permute-start) | collective-permute-done | bytes 294944 | tf_op jit(solution)/shard_map/while/body/eval_jaxpr/ppermute | solution.py:13
  584.6 9.2 %collective-permute-done = f32[128,576]{0,1:T(8,128)S(1)} collective-permute-done((f32[128,576]{0,1:T(8,128)S(1)}, f32[128,576]{0,1:T(8,128)S(1)}, u32[]{:S(2)}, u32[]{:S(2)}) %collective-permute-start) | collective-permute-done | bytes 294944 | tf_op jit(solution)/shard_map/while/body/eval_jaxpr/ppermute | solution.py:13
  600.5 9.2 %collective-permute-done = f32[128,576]{0,1:T(8,128)S(1)} collective-permute-done((f32[128,576]{0,1:T(8,128)S(1)}, f32[128,576]{0,1:T(8,128)S(1)}, u32[]{:S(2)}, u32[]{:S(2)}) %collective-permute-start) | collective-permute-done | bytes 294944 | tf_op jit(solution)/shard_map/while/body/eval_jaxpr/ppermute | solution.py:13
  616.5 9.2 %collective-permute-done = f32[128,576]{0,1:T(8,128)S(1)} collective-permute-done((f32[128,576]{0,1:T(8,128)S(1)}, f32[128,576]{0,1:T(8,128)S(1)}, u32[]{:S(2)}, u32[]{:S(2)}) %collective-permute-start) | collective-permute-done | bytes 294944 | tf_op jit(solution)/shard_map/while/body/eval_jaxpr/ppermute | solution.py:13
  630.8 147.4 %all-reduce.5.cloned.1.call-done = f32[128,576]{1,0:T(8,128)} async-done(((f32[128,576]{1,0:T(8,128)}), f32[128,576]{1,0:T(8,128)}) %all-reduce.5.cloned.1.call-update) | async-done | bytes 294928
  (285 shorter events, 243.0 us)
Async XLA Ops:
  11.3 121.7 %all-to-all-start = ((bf16[32,128,576]{1,2,0:T(8,128)(2,1)}), bf16[32,128,576]{1,2,0:T(8,128)(2,1)}, u32[]{:S(2)}, u32[]{:S(2)}) async-start(bf16[32,128,576]{1,2,0:T(8,128)(2,1)} %stack.2), calls=%async_computation | async-start | bytes 9437184 | tf_op jit(solution)/shard_map/all_to_all | solution.py:82
  24.9 753.2 %all-reduce.5.cloned.1.call-start = ((), (), s32[]{:S(2)}) async-start(), calls=%async_computation.1 | async-start | bytes 655360
  158.7 8.0 %collective-permute-start = (f32[128,576]{0,1:T(8,128)S(1)}, f32[128,576]{0,1:T(8,128)S(1)}, u32[]{:S(2)}, u32[]{:S(2)}) collective-permute-start(f32[128,576]{0,1:T(8,128)S(1)} %fusion.96), channel_id=1, source_target_pairs={{496,0},{0,16},{16,32},{32,48},{48,64},{64,80},{80,96},{96,112},{1... | collective-permute-start | bytes 884744 | tf_op jit(solution)/shard_map/while/body/eval_jaxpr/ppermute | solution.py:13
  170.3 8.8 %collective-permute-start = (f32[128,576]{0,1:T(8,128)S(1)}, f32[128,576]{0,1:T(8,128)S(1)}, u32[]{:S(2)}, u32[]{:S(2)}) collective-permute-start(f32[128,576]{0,1:T(8,128)S(1)} %fusion.96), channel_id=1, source_target_pairs={{496,0},{0,16},{16,32},{32,48},{48,64},{64,80},{80,96},{96,112},{1... | collective-permute-start | bytes 884744 | tf_op jit(solution)/shard_map/while/body/eval_jaxpr/ppermute | solution.py:13
  182.7 13.7 %collective-permute-start = (f32[128,576]{0,1:T(8,128)S(1)}, f32[128,576]{0,1:T(8,128)S(1)}, u32[]{:S(2)}, u32[]{:S(2)}) collective-permute-start(f32[128,576]{0,1:T(8,128)S(1)} %fusion.96), channel_id=1, source_target_pairs={{496,0},{0,16},{16,32},{32,48},{48,64},{64,80},{80,96},{96,112},{1... | collective-permute-start | bytes 884744 | tf_op jit(solution)/shard_map/while/body/eval_jaxpr/ppermute | solution.py:13
  200.0 12.3 %collective-permute-start = (f32[128,576]{0,1:T(8,128)S(1)}, f32[128,576]{0,1:T(8,128)S(1)}, u32[]{:S(2)}, u32[]{:S(2)}) collective-permute-start(f32[128,576]{0,1:T(8,128)S(1)} %fusion.96), channel_id=1, source_target_pairs={{496,0},{0,16},{16,32},{32,48},{48,64},{64,80},{80,96},{96,112},{1... | collective-permute-start | bytes 884744 | tf_op jit(solution)/shard_map/while/body/eval_jaxpr/ppermute | solution.py:13
  215.8 12.3 %collective-permute-start = (f32[128,576]{0,1:T(8,128)S(1)}, f32[128,576]{0,1:T(8,128)S(1)}, u32[]{:S(2)}, u32[]{:S(2)}) collective-permute-start(f32[128,576]{0,1:T(8,128)S(1)} %fusion.96), channel_id=1, source_target_pairs={{496,0},{0,16},{16,32},{32,48},{48,64},{64,80},{80,96},{96,112},{1... | collective-permute-start | bytes 884744 | tf_op jit(solution)/shard_map/while/body/eval_jaxpr/ppermute | solution.py:13
  231.7 12.3 %collective-permute-start = (f32[128,576]{0,1:T(8,128)S(1)}, f32[128,576]{0,1:T(8,128)S(1)}, u32[]{:S(2)}, u32[]{:S(2)}) collective-permute-start(f32[128,576]{0,1:T(8,128)S(1)} %fusion.96), channel_id=1, source_target_pairs={{496,0},{0,16},{16,32},{32,48},{48,64},{64,80},{80,96},{96,112},{1... | collective-permute-start | bytes 884744 | tf_op jit(solution)/shard_map/while/body/eval_jaxpr/ppermute | solution.py:13
  247.5 12.3 %collective-permute-start = (f32[128,576]{0,1:T(8,128)S(1)}, f32[128,576]{0,1:T(8,128)S(1)}, u32[]{:S(2)}, u32[]{:S(2)}) collective-permute-start(f32[128,576]{0,1:T(8,128)S(1)} %fusion.96), channel_id=1, source_target_pairs={{496,0},{0,16},{16,32},{32,48},{48,64},{64,80},{80,96},{96,112},{1... | collective-permute-start | bytes 884744 | tf_op jit(solution)/shard_map/while/body/eval_jaxpr/ppermute | solution.py:13
  263.4 12.3 %collective-permute-start = (f32[128,576]{0,1:T(8,128)S(1)}, f32[128,576]{0,1:T(8,128)S(1)}, u32[]{:S(2)}, u32[]{:S(2)}) collective-permute-start(f32[128,576]{0,1:T(8,128)S(1)} %fusion.96), channel_id=1, source_target_pairs={{496,0},{0,16},{16,32},{32,48},{48,64},{64,80},{80,96},{96,112},{1... | collective-permute-start | bytes 884744 | tf_op jit(solution)/shard_map/while/body/eval_jaxpr/ppermute | solution.py:13
  279.2 12.3 %collective-permute-start = (f32[128,576]{0,1:T(8,128)S(1)}, f32[128,576]{0,1:T(8,128)S(1)}, u32[]{:S(2)}, u32[]{:S(2)}) collective-permute-start(f32[128,576]{0,1:T(8,128)S(1)} %fusion.96), channel_id=1, source_target_pairs={{496,0},{0,16},{16,32},{32,48},{48,64},{64,80},{80,96},{96,112},{1... | collective-permute-start | bytes 884744 | tf_op jit(solution)/shard_map/while/body/eval_jaxpr/ppermute | solution.py:13
  295.1 12.3 %collective-permute-start = (f32[128,576]{0,1:T(8,128)S(1)}, f32[128,576]{0,1:T(8,128)S(1)}, u32[]{:S(2)}, u32[]{:S(2)}) collective-permute-start(f32[128,576]{0,1:T(8,128)S(1)} %fusion.96), channel_id=1, source_target_pairs={{496,0},{0,16},{16,32},{32,48},{48,64},{64,80},{80,96},{96,112},{1... | collective-permute-start | bytes 884744 | tf_op jit(solution)/shard_map/while/body/eval_jaxpr/ppermute | solution.py:13
  310.9 12.3 %collective-permute-start = (f32[128,576]{0,1:T(8,128)S(1)}, f32[128,576]{0,1:T(8,128)S(1)}, u32[]{:S(2)}, u32[]{:S(2)}) collective-permute-start(f32[128,576]{0,1:T(8,128)S(1)} %fusion.96), channel_id=1, source_target_pairs={{496,0},{0,16},{16,32},{32,48},{48,64},{64,80},{80,96},{96,112},{1... | collective-permute-start | bytes 884744 | tf_op jit(solution)/shard_map/while/body/eval_jaxpr/ppermute | solution.py:13
  326.8 12.3 %collective-permute-start = (f32[128,576]{0,1:T(8,128)S(1)}, f32[128,576]{0,1:T(8,128)S(1)}, u32[]{:S(2)}, u32[]{:S(2)}) collective-permute-start(f32[128,576]{0,1:T(8,128)S(1)} %fusion.96), channel_id=1, source_target_pairs={{496,0},{0,16},{16,32},{32,48},{48,64},{64,80},{80,96},{96,112},{1... | collective-permute-start | bytes 884744 | tf_op jit(solution)/shard_map/while/body/eval_jaxpr/ppermute | solution.py:13
  342.6 12.3 %collective-permute-start = (f32[128,576]{0,1:T(8,128)S(1)}, f32[128,576]{0,1:T(8,128)S(1)}, u32[]{:S(2)}, u32[]{:S(2)}) collective-permute-start(f32[128,576]{0,1:T(8,128)S(1)} %fusion.96), channel_id=1, source_target_pairs={{496,0},{0,16},{16,32},{32,48},{48,64},{64,80},{80,96},{96,112},{1... | collective-permute-start | bytes 884744 | tf_op jit(solution)/shard_map/while/body/eval_jaxpr/ppermute | solution.py:13
  358.4 12.3 %collective-permute-start = (f32[128,576]{0,1:T(8,128)S(1)}, f32[128,576]{0,1:T(8,128)S(1)}, u32[]{:S(2)}, u32[]{:S(2)}) collective-permute-start(f32[128,576]{0,1:T(8,128)S(1)} %fusion.96), channel_id=1, source_target_pairs={{496,0},{0,16},{16,32},{32,48},{48,64},{64,80},{80,96},{96,112},{1... | collective-permute-start | bytes 884744 | tf_op jit(solution)/shard_map/while/body/eval_jaxpr/ppermute | solution.py:13
  374.3 12.3 %collective-permute-start = (f32[128,576]{0,1:T(8,128)S(1)}, f32[128,576]{0,1:T(8,128)S(1)}, u32[]{:S(2)}, u32[]{:S(2)}) collective-permute-start(f32[128,576]{0,1:T(8,128)S(1)} %fusion.96), channel_id=1, source_target_pairs={{496,0},{0,16},{16,32},{32,48},{48,64},{64,80},{80,96},{96,112},{1... | collective-permute-start | bytes 884744 | tf_op jit(solution)/shard_map/while/body/eval_jaxpr/ppermute | solution.py:13
  390.1 12.3 %collective-permute-start = (f32[128,576]{0,1:T(8,128)S(1)}, f32[128,576]{0,1:T(8,128)S(1)}, u32[]{:S(2)}, u32[]{:S(2)}) collective-permute-start(f32[128,576]{0,1:T(8,128)S(1)} %fusion.96), channel_id=1, source_target_pairs={{496,0},{0,16},{16,32},{32,48},{48,64},{64,80},{80,96},{96,112},{1... | collective-permute-start | bytes 884744 | tf_op jit(solution)/shard_map/while/body/eval_jaxpr/ppermute | solution.py:13
  406.0 12.4 %collective-permute-start = (f32[128,576]{0,1:T(8,128)S(1)}, f32[128,576]{0,1:T(8,128)S(1)}, u32[]{:S(2)}, u32[]{:S(2)}) collective-permute-start(f32[128,576]{0,1:T(8,128)S(1)} %fusion.96), channel_id=1, source_target_pairs={{496,0},{0,16},{16,32},{32,48},{48,64},{64,80},{80,96},{96,112},{1... | collective-permute-start | bytes 884744 | tf_op jit(solution)/shard_map/while/body/eval_jaxpr/ppermute | solution.py:13
  422.0 12.4 %collective-permute-start = (f32[128,576]{0,1:T(8,128)S(1)}, f32[128,576]{0,1:T(8,128)S(1)}, u32[]{:S(2)}, u32[]{:S(2)}) collective-permute-start(f32[128,576]{0,1:T(8,128)S(1)} %fusion.96), channel_id=1, source_target_pairs={{496,0},{0,16},{16,32},{32,48},{48,64},{64,80},{80,96},{96,112},{1... | collective-permute-start | bytes 884744 | tf_op jit(solution)/shard_map/while/body/eval_jaxpr/ppermute | solution.py:13
  437.9 12.4 %collective-permute-start = (f32[128,576]{0,1:T(8,128)S(1)}, f32[128,576]{0,1:T(8,128)S(1)}, u32[]{:S(2)}, u32[]{:S(2)}) collective-permute-start(f32[128,576]{0,1:T(8,128)S(1)} %fusion.96), channel_id=1, source_target_pairs={{496,0},{0,16},{16,32},{32,48},{48,64},{64,80},{80,96},{96,112},{1... | collective-permute-start | bytes 884744 | tf_op jit(solution)/shard_map/while/body/eval_jaxpr/ppermute | solution.py:13
  453.9 12.4 %collective-permute-start = (f32[128,576]{0,1:T(8,128)S(1)}, f32[128,576]{0,1:T(8,128)S(1)}, u32[]{:S(2)}, u32[]{:S(2)}) collective-permute-start(f32[128,576]{0,1:T(8,128)S(1)} %fusion.96), channel_id=1, source_target_pairs={{496,0},{0,16},{16,32},{32,48},{48,64},{64,80},{80,96},{96,112},{1... | collective-permute-start | bytes 884744 | tf_op jit(solution)/shard_map/while/body/eval_jaxpr/ppermute | solution.py:13
  469.8 12.4 %collective-permute-start = (f32[128,576]{0,1:T(8,128)S(1)}, f32[128,576]{0,1:T(8,128)S(1)}, u32[]{:S(2)}, u32[]{:S(2)}) collective-permute-start(f32[128,576]{0,1:T(8,128)S(1)} %fusion.96), channel_id=1, source_target_pairs={{496,0},{0,16},{16,32},{32,48},{48,64},{64,80},{80,96},{96,112},{1... | collective-permute-start | bytes 884744 | tf_op jit(solution)/shard_map/while/body/eval_jaxpr/ppermute | solution.py:13
  485.8 12.4 %collective-permute-start = (f32[128,576]{0,1:T(8,128)S(1)}, f32[128,576]{0,1:T(8,128)S(1)}, u32[]{:S(2)}, u32[]{:S(2)}) collective-permute-start(f32[128,576]{0,1:T(8,128)S(1)} %fusion.96), channel_id=1, source_target_pairs={{496,0},{0,16},{16,32},{32,48},{48,64},{64,80},{80,96},{96,112},{1... | collective-permute-start | bytes 884744 | tf_op jit(solution)/shard_map/while/body/eval_jaxpr/ppermute | solution.py:13
  501.7 12.4 %collective-permute-start = (f32[128,576]{0,1:T(8,128)S(1)}, f32[128,576]{0,1:T(8,128)S(1)}, u32[]{:S(2)}, u32[]{:S(2)}) collective-permute-start(f32[128,576]{0,1:T(8,128)S(1)} %fusion.96), channel_id=1, source_target_pairs={{496,0},{0,16},{16,32},{32,48},{48,64},{64,80},{80,96},{96,112},{1... | collective-permute-start | bytes 884744 | tf_op jit(solution)/shard_map/while/body/eval_jaxpr/ppermute | solution.py:13
  517.7 12.4 %collective-permute-start = (f32[128,576]{0,1:T(8,128)S(1)}, f32[128,576]{0,1:T(8,128)S(1)}, u32[]{:S(2)}, u32[]{:S(2)}) collective-permute-start(f32[128,576]{0,1:T(8,128)S(1)} %fusion.96), channel_id=1, source_target_pairs={{496,0},{0,16},{16,32},{32,48},{48,64},{64,80},{80,96},{96,112},{1... | collective-permute-start | bytes 884744 | tf_op jit(solution)/shard_map/while/body/eval_jaxpr/ppermute | solution.py:13
  533.6 12.4 %collective-permute-start = (f32[128,576]{0,1:T(8,128)S(1)}, f32[128,576]{0,1:T(8,128)S(1)}, u32[]{:S(2)}, u32[]{:S(2)}) collective-permute-start(f32[128,576]{0,1:T(8,128)S(1)} %fusion.96), channel_id=1, source_target_pairs={{496,0},{0,16},{16,32},{32,48},{48,64},{64,80},{80,96},{96,112},{1... | collective-permute-start | bytes 884744 | tf_op jit(solution)/shard_map/while/body/eval_jaxpr/ppermute | solution.py:13
  549.5 12.4 %collective-permute-start = (f32[128,576]{0,1:T(8,128)S(1)}, f32[128,576]{0,1:T(8,128)S(1)}, u32[]{:S(2)}, u32[]{:S(2)}) collective-permute-start(f32[128,576]{0,1:T(8,128)S(1)} %fusion.96), channel_id=1, source_target_pairs={{496,0},{0,16},{16,32},{32,48},{48,64},{64,80},{80,96},{96,112},{1... | collective-permute-start | bytes 884744 | tf_op jit(solution)/shard_map/while/body/eval_jaxpr/ppermute | solution.py:13
  565.5 12.4 %collective-permute-start = (f32[128,576]{0,1:T(8,128)S(1)}, f32[128,576]{0,1:T(8,128)S(1)}, u32[]{:S(2)}, u32[]{:S(2)}) collective-permute-start(f32[128,576]{0,1:T(8,128)S(1)} %fusion.96), channel_id=1, source_target_pairs={{496,0},{0,16},{16,32},{32,48},{48,64},{64,80},{80,96},{96,112},{1... | collective-permute-start | bytes 884744 | tf_op jit(solution)/shard_map/while/body/eval_jaxpr/ppermute | solution.py:13
  581.4 12.4 %collective-permute-start = (f32[128,576]{0,1:T(8,128)S(1)}, f32[128,576]{0,1:T(8,128)S(1)}, u32[]{:S(2)}, u32[]{:S(2)}) collective-permute-start(f32[128,576]{0,1:T(8,128)S(1)} %fusion.96), channel_id=1, source_target_pairs={{496,0},{0,16},{16,32},{32,48},{48,64},{64,80},{80,96},{96,112},{1... | collective-permute-start | bytes 884744 | tf_op jit(solution)/shard_map/while/body/eval_jaxpr/ppermute | solution.py:13
  597.4 12.4 %collective-permute-start = (f32[128,576]{0,1:T(8,128)S(1)}, f32[128,576]{0,1:T(8,128)S(1)}, u32[]{:S(2)}, u32[]{:S(2)}) collective-permute-start(f32[128,576]{0,1:T(8,128)S(1)} %fusion.96), channel_id=1, source_target_pairs={{496,0},{0,16},{16,32},{32,48},{48,64},{64,80},{80,96},{96,112},{1... | collective-permute-start | bytes 884744 | tf_op jit(solution)/shard_map/while/body/eval_jaxpr/ppermute | solution.py:13
  613.3 12.4 %collective-permute-start = (f32[128,576]{0,1:T(8,128)S(1)}, f32[128,576]{0,1:T(8,128)S(1)}, u32[]{:S(2)}, u32[]{:S(2)}) collective-permute-start(f32[128,576]{0,1:T(8,128)S(1)} %fusion.96), channel_id=1, source_target_pairs={{496,0},{0,16},{16,32},{32,48},{48,64},{64,80},{80,96},{96,112},{1... | collective-permute-start | bytes 884744 | tf_op jit(solution)/shard_map/while/body/eval_jaxpr/ppermute | solution.py:13
  (6 other events, 271.3 us)
Sparse Core Ops, SparseCore 0:
  626.9 151.2 all-reduce.4
